TPU v7x, 768 devices: a whole 4x8x12 slice. The times are simulated.
768 devices in a mesh: row: 32 (over z_hi, x, core), col: 24 (over z_lo, y).
Axes of the slice: x: 4, y: 8, z: 12 (z_hi: 4, z_lo: 3; z = z_hi * 3 + z_lo), core: 2. Of those that a mesh axis runs over, the one named last changes fastest.
Arguments:
- inverse_tiles: float32 [12288, 12288], P('row', 'col'), may hold values from -0.078125 to 0.078125
- factor_panels: float32 [3, 512, 6144], P(None, 'row', 'col'), may hold values from -6 to 6
- block_rows: int32 [3, 192], replicated, may hold values from 0 to 383, as said below
- couplings: float32 [2, 512, 512], replicated, may hold values from -0.25 to 0.25
Outputs:
- new_columns: float32 [3, 12288, 512], P(None, ('row', 'col'))
Inputs may be any that keep to these rules, and one draw needn't show every extreme that they name: `block_rows`: each row lists 192 different row blocks in no particular order; in each row, all 16 blocks q * 16 to q * 16 + 15 of some q are listed.
All inputs are finite; a program needn't handle non-finite values.
Results may differ from a plain program's by a relative error of at most 0.0001.
Values sent between devices are 32-bit elements; how exact they have to be, the bound alone decides.
A program may use at most 32 MiB of HBM per device.

v0:
```python
import jax
import jax.numpy as jnp
from jax import lax
from jax.sharding import PartitionSpec as P


def on_device(inverse_tiles, factor_panels, block_rows, couplings):
    tile_rows, tile_cols = inverse_tiles.shape
    piece_rows = factor_panels.shape[1]
    listed = block_rows.shape[1]
    col_count = lax.axis_size("col")
    block_size = factor_panels.shape[2] * col_count // listed
    local_blocks = tile_cols // block_size
    my_column = lax.axis_index("col")
    offset = my_column * local_blocks
    targets = offset + jnp.arange(local_blocks, dtype=jnp.int32)
    results = []
    previous = None
    for section in range(factor_panels.shape[0]):
        section_rows = block_rows[section]
        gathered = lax.all_gather(factor_panels[section], "col", axis=1, tiled=True)
        onehot = (section_rows[:, None] == targets[None, :]).astype(jnp.float32)
        picked = jnp.einsum(
            "wpr,pq->wqr",
            gathered.reshape(piece_rows, listed, block_size),
            onehot,
            precision=lax.Precision.HIGHEST,
        ).reshape(piece_rows, tile_cols)
        partial_value = lax.dot_general(
            inverse_tiles,
            lax.all_gather(picked, "row", axis=0, tiled=True),
            (((1,), (1,)), ((), ())),
            precision=lax.Precision.HIGHEST,
            preferred_element_type=jnp.float32,
        )
        summed = lax.psum_scatter(partial_value, "col", scatter_dimension=0, tiled=True)
        if previous is not None:
            summed = summed + jnp.dot(
                previous,
                couplings[section - 1],
                precision=lax.Precision.HIGHEST,
                preferred_element_type=jnp.float32,
            )
        previous = -summed
        results.append(previous)
    return jnp.stack(results)


def solution(mesh):
    return jax.shard_map(
        on_device,
        mesh=mesh,
        in_specs=(P("row", "col"), P(None, "row", "col"), P(), P()),
        out_specs=P(None, ("row", "col"), None),
        check_vma=False,
    )
```

profile of v0, /device:TPU:192, one launch (start us, length us, event | category | flops | bytes accessed | tf_op | source)
XLA Modules:
  0.0 673.5 jit_solution(3066413539699991528)
XLA Ops:
  6.5 0.0 copy-start
  6.5 0.0 all-gather.7.cloned.1.call-start
  6.5 0.8 fusion.20
  7.4 0.8 fusion.21
  8.2 67.0 %all-gather = f32[1,16,6144]{2,1,0:T(8,128)S(1)} all-gather(f32[1,16,256]{2,1,0:T(8,128)S(1)} %get-tuple-element.5), channel_id=2, replica_groups=mesh['row'=32,'col'=24] {'col'}, dimensions={2}, use_global_device_ids=true | all-gather | bytes 409600 | tf_op jit(solution)/shard_map/all_gather | solution.py:21
  75.2 0.5 reshape.25
  75.7 0.6 convolution_bitcast_fusion.5
  76.3 0.7 reshape.26
  77.1 0.0 all-gather.7.cloned.1.call-update
  77.1 0.0 all-gather.9.cloned.1.call-start
  77.1 60.0 %all-gather.1 = f32[1,16,6144]{2,1,0:T(8,128)S(1)} all-gather(f32[1,16,256]{2,1,0:T(8,128)S(1)} %get-tuple-element.7), channel_id=3, replica_groups=mesh['row'=32,'col'=24] {'col'}, dimensions={2}, use_global_device_ids=true | all-gather | bytes 409600 | tf_op jit(solution)/shard_map/all_gather | solution.py:21
  137.1 0.5 reshape.27
  137.6 0.6 convolution_bitcast_fusion.4
  138.3 0.7 reshape.28
  139.0 0.0 all-gather.9.cloned.1.call-update
  139.0 0.0 all-gather.11.cloned.1.call-start
  139.1 60.8 %all-gather.2 = f32[1,16,6144]{2,1,0:T(8,128)S(1)} all-gather(f32[1,16,256]{2,1,0:T(8,128)S(1)} %get-tuple-element.6), channel_id=4, replica_groups=mesh['row'=32,'col'=24] {'col'}, dimensions={2}, use_global_device_ids=true | all-gather | bytes 409600 | tf_op jit(solution)/shard_map/all_gather | solution.py:21
  199.8 0.5 reshape.29
  200.4 0.6 convolution_bitcast_fusion.3
  201.0 0.7 reshape.30
  201.7 0.0 all-gather.11.cloned.1.call-update
  201.7 0.0 reduce-scatter.10.cloned.1.call-start
  201.8 0.0 all-gather.7.cloned.1.call-done
  201.8 0.0 copy-done
  201.8 3.0 convolution_bitcast_fusion.2
  204.9 1.2 copy.23
  206.0 0.0 reduce-scatter.10.cloned.1.call-update
  206.0 0.0 reduce-scatter.12.cloned.1.call-start
  206.1 1.5 all-gather.9.cloned.1.call-done
  207.6 3.0 convolution_bitcast_fusion.1
  210.6 1.2 copy.25
  211.8 0.0 reduce-scatter.12.cloned.1.call-update
  211.9 0.2 reduce-scatter.14.cloned.1.call-start
  212.1 63.7 %all-gather.11.cloned.1.call-done = f32[512,512]{1,0:T(8,128)} async-done(((f32[16,512]{1,0:T(8,128)}), f32[512,512]{1,0:T(8,128)}) %all-gather.11.cloned.1.call-update) | async-done | bytes 1048592 | tf_op jit(solution)/shard_map/all_gather | solution.py:31
  275.8 3.0 convolution_bitcast_fusion
  278.9 1.2 copy.27
  280.0 0.0 copy-start.1
  280.0 0.0 reduce-scatter.14.cloned.1.call-update
  280.1 128.7 %reduce-scatter.10.cloned.1.call-done = f32[16,512]{1,0:T(8,128)} async-done(((f32[384,512]{1,0:T(8,128)}), f32[16,512]{1,0:T(8,128)}) %reduce-scatter.10.cloned.1.call-update) | async-done | bytes 32784
  408.7 0.9 copy.24
  409.6 0.1 copy.19
  409.7 127.1 %reduce-scatter.12.cloned.1.call-done = f32[16,512]{1,0:T(8,128)} async-done(((f32[384,512]{1,0:T(8,128)}), f32[16,512]{1,0:T(8,128)}) %reduce-scatter.12.cloned.1.call-update) | async-done | bytes 32784 | tf_op jit(solution)/shard_map/reduce_scatter | solution.py:36
  536.8 1.9 fusion.2
  538.7 126.0 %reduce-scatter.14.cloned.1.call-done = f32[16,512]{1,0:T(8,128)} async-done(((f32[384,512]{1,0:T(8,128)}), f32[16,512]{1,0:T(8,128)}) %reduce-scatter.14.cloned.1.call-update) | async-done | bytes 32784 | tf_op jit(solution)/shard_map/reduce_scatter | solution.py:36
  664.7 0.0 copy-done.1
  664.7 1.4 fusion.1
  666.0 0.6 pad_maximum_fusion
  (2 shorter events, 0.0 us)
Async XLA Ops:
  6.5 195.3 %copy-start = (f32[384,512]{1,0:T(8,128)S(1)}, f32[384,512]{1,0:T(8,128)}, u32[]{:S(2)}) copy-start(f32[384,512]{1,0:T(8,128)} %param.4) | copy-start | bytes 2359300
  6.5 195.3 %all-gather.7.cloned.1.call-start = ((), (), s32[]{:S(2)}) async-start(), calls=%async_computation.3 | async-start | bytes 1081344 | tf_op jit(solution)/shard_map/all_gather | solution.py:31
  77.1 130.5 %all-gather.9.cloned.1.call-start = ((), (), s32[]{:S(2)}) async-start(), calls=%async_computation.4 | async-start | bytes 1081344 | tf_op jit(solution)/shard_map/all_gather | solution.py:31
  139.0 136.8 %all-gather.11.cloned.1.call-start = ((), (), s32[]{:S(2)}) async-start(), calls=%async_computation.5 | async-start | bytes 1081344 | tf_op jit(solution)/shard_map/all_gather | solution.py:31
  201.7 207.0 %reduce-scatter.10.cloned.1.call-start = ((), (), s32[]{:S(2)}) async-start(), calls=%async_computation.6 | async-start | bytes 819200
  206.0 330.8 %reduce-scatter.12.cloned.1.call-start = ((), (), s32[]{:S(2)}) async-start(), calls=%async_computation.7 | async-start | bytes 819200 | tf_op jit(solution)/shard_map/reduce_scatter | solution.py:36
  211.9 452.8 %reduce-scatter.14.cloned.1.call-start = ((), (), s32[]{:S(2)}) async-start(), calls=%async_computation.8 | async-start | bytes 819200 | tf_op jit(solution)/shard_map/reduce_scatter | solution.py:36
  280.0 384.6 %copy-start.1 = (f32[2,512,512]{2,1,0:T(8,128)S(1)}, f32[2,512,512]{2,1,0:T(8,128)}, u32[]{:S(2)}) copy-start(f32[2,512,512]{2,1,0:T(8,128)} %param.7) | copy-start | bytes 6291460
Sparse Core Ops, SparseCore 0:
  77.2 62.0 all-gather.6
  143.0 64.5 all-gather.8
  211.3 64.4 all-gather.10
  278.8 129.9 reduce-scatter.9
  412.0 124.7 reduce-scatter.11
  539.8 124.8 reduce-scatter.13
where the time goes:
time: 674 us
  waiting for transfers between devices  447 us (66%)
  blocking collectives  188 us (28%)
  matrix products  14.2 us (2%)
  between operations  13.6 us (2%)
  local copies, waits for them, and re-layouts  9.82 us (1%)
    reduce_scatter x2, waiting for transfers between devices, on_device(): lax.psum_scatter(partial_value, 'col', scatter_dimension=0, tiled=True)  253 us
    all_gather x3, blocking collectives, on_device(): gathered = lax.all_gather(factor_panels[section], 'col', axis=1, tiled=True)  188 us
    unnamed x7, waiting for transfers between devices  129 us
    all_gather x3, waiting for transfers between devices, on_device(): lax.all_gather(picked, 'row', axis=0, tiled=True)  65.2 us
  transfers between devices with their start and end apart: 6, of which 5 were waited for; matrix products, arithmetic and copies ran while one was open for 3% of the time, Pallas kernels for 0%

commit v1 on v0

v1 whole, which is shorter than its diff:
```python
import jax
import jax.numpy as jnp
from jax import lax
from jax.experimental import pallas as pl
from jax.experimental.pallas import tpu as pltpu
from jax.sharding import PartitionSpec as P

ZH, X, CORE, ZL, Y = 4, 4, 2, 3, 8
S, W, RB, NBC, NZB = 3, 512, 32, 16, 192
WP = W // (ZH * X * CORE)
LISTED = NZB // (ZL * Y)
ROWS, DEPTH = 384, 512
OUT = ROWS // (ZL * Y)
TARGETS = ZL * NBC
QUAD = 128 // RB
MESH = pl.DeviceIdType.MESH
F32, BF16 = jnp.float32, jnp.bfloat16
COPIES = 256
GROUPS = ((4,), (3, -3), (2, -2), (1, -1), (0,))
Z_FIRST = (2,)
ORDER = (
    (1, 0), (1, 1), (0,), (1, 2), (2, 0), (2, 1), (3, 0), (2, 2), (3, 1), (4, 0, 2), (3, 2), (4, 0, 3),
    (4, 0, 1), (5, 0, 0), (4, 1, 2), (4, 1, 3), (4, 1, 1), (5, 1, 0), (5, 0, 2), (5, 0, 1), (5, 0, -1),
    (4, 2, 2), (4, 2, 1), (4, 2, 3), (5, 2, 0), (6, 0), (5, 1, 2), (5, 1, 1), (5, 1, -1), (6, 1),
    (8, 0, 1, 0), (8, 0, 0, 0), (5, 2, 2), (8, 0, 2, 0), (5, 2, -1), (5, 2, 1), (6, 2), (8, 1, 1, 0),
    (8, 1, 0, 0), (8, 0, 1, 1), (8, 1, 2, 0), (8, 0, 0, 1), (8, 0, 2, 1), (7, 2, 0), (8, 1, 1, 1),
    (8, 1, 0, 1), (7, 2, 1), (8, 0, 1, 2), (8, 1, 2, 1), (7, 2, 2), (8, 0, 0, 2), (8, 0, 2, 2), (8, 2, 2, 0),
    (7, 2, 3), (8, 1, 1, 2), (7, 2, 4), (8, 1, 0, 2), (8, 0, 1, 3), (8, 1, 2, 2), (8, 0, 0, 3), (8, 0, 2, 3),
    (8, 2, 2, 1), (8, 1, 1, 3), (8, 1, 0, 3), (8, 1, 2, 3), (9, 0), (8, 2, 2, 2), (9, 1), (8, 2, 2, 3),
    (9, 2),
)


def split(value):
    high = value.astype(BF16)
    return high, (value - high.astype(F32)).astype(BF16)


def dot3(a_high, a_low, b_high, b_low, dims):
    def one(a, b):
        return lax.dot_general(a, b, (dims, ((), ())), preferred_element_type=F32)

    return one(a_high, b_high) + (one(a_high, b_low) + one(a_low, b_high))


def kernel(
    table, a_hbm, f_ref, k_hbm, o_ref,
    a_ref, k_ref, f_own, listed_0, listed_1, listed_2, picked, from_zl, factor, partial,
    half_in, step_in, whole_in, last_in, a_high, a_low, k_high, k_low, fill_sem, send_sem, recv_sem,
):
    row, col = lax.axis_index("row"), lax.axis_index("col")
    zh, x, core = row // (X * CORE), lax.rem(row // CORE, X), lax.rem(row, CORE)
    zl, y = col // Y, lax.rem(col, Y)
    listed = (listed_0, listed_1, listed_2)

    def turn(value, by, size):
        return lax.rem(value + (by + size), size)

    def device(dzh=0, dx=0, dcore=0, dzl=0, dy=0):
        at_row = (turn(zh, dzh, ZH) * X + turn(x, dx, X)) * CORE + (1 - core if dcore else core)
        return (at_row, turn(zl, dzl, ZL) * Y + turn(y, dy, Y))

    fill_a = pltpu.make_async_copy(a_hbm, a_ref, fill_sem.at[0])
    fill_k = pltpu.make_async_copy(k_hbm, k_ref, fill_sem.at[1])
    fill_a.start()
    fill_k.start()

    barrier = pltpu.get_barrier_semaphore()
    partners = (
        [dict(dy=o) for o in range(1, Y)]
        + [dict(dzl=o) for o in range(1, ZL)]
        + [dict(dzh=o) for o in range(1, ZH)]
        + [dict(dx=1), dict(dx=-1), dict(dx=2), dict(dcore=1)]
    )
    for partner in partners:
        pl.semaphore_signal(barrier, inc=1, device_id=device(**partner), device_id_type=MESH)
    for s in range(S):
        for h in range(2):
            f_own[s, h] = f_ref[s, :, h * 128 : (h + 1) * 128]
            listed[s][y, h] = f_ref[s, :, h * 128 : (h + 1) * 128]
    pl.semaphore_wait(barrier, len(partners))

    ids, unsent = {}, []

    def copy(key, source, target, to):
        at = ids.setdefault(key, len(ids))
        return pltpu.make_async_remote_copy(
            src_ref=source, dst_ref=target, send_sem=send_sem.at[at], recv_sem=recv_sem.at[at],
            device_id=to, device_id_type=MESH,
        )

    def send(key, source, target, **to):
        made = copy(key, source, target, device(**to))
        made.start()
        unsent.append(made)

    def arrive(key, landed, **to):
        copy(key, landed, landed, device(**to)).wait_recv()

    lane_block = lax.broadcasted_iota(jnp.int32, (WP, 128), 1) // RB

    def gather_y(s):
        for o in (4, 3, 5, 2, 6, 1, 7):
            send(("y", s, o), f_own.at[s], listed[s].at[y], dy=o)

    def pick(s):
        for o in range(1, Y):
            arrive(("y", s, o), listed[s].at[turn(y, -o, Y)], dy=o)
        for part in range(ZL):
            for quad in range(NBC // QUAD):
                value = jnp.zeros((WP, 128), F32)
                for q in range(QUAD):
                    at = (s * TARGETS + part * NBC + quad * QUAD + q) * 3
                    source, shift, place = table[at], table[at + 1], table[at + 2]
                    block = pltpu.roll(listed[s][source // 2, lax.rem(source, 2)], shift, 1)
                    value = jnp.where(lane_block == place, block, value)
                picked[s, part, :, quad * 128 : (quad + 1) * 128] = value
        for o in (1, 2):
            send(("l", s, o), picked.at[s, turn(zl, o, ZL)], from_zl.at[s, o - 1], dzl=o)

    def own(s):
        for o in (1, 2):
            arrive(("l", s, o), from_zl.at[s, o - 1], dzl=o)
        factor[s, zh, x, core] = picked[s, zl] + (from_zl[s, 0] + from_zl[s, 1])
        piece = factor.at[s, zh, x, core]
        for o in (2, 1, 3):
            send(("h", s, o), piece, piece, dzh=o)
        along_x(s, 0)

    def along_x(s, o):
        piece = factor.at[s, turn(zh, -o, ZH), x, core]
        for by in (2, 1, -1):
            send(("x", s, o, by), piece, piece, dx=by)

    def from_zh(s, o):
        arrive(("h", s, o), factor.at[s, turn(zh, -o, ZH), x, core], dzh=o)
        along_x(s, o)

    def to_core(s, by):
        for o in range(ZH) if by else ():
            arrive(("x", s, o, by), factor.at[s, turn(zh, -o, ZH), turn(x, -by, X), core], dx=by)
        piece = factor.at[s, :, turn(x, -by, X), core]
        send(("c", s, by), piece, piece, dcore=1)

    def multiply(s):
        for by in (0, 1, -1, 2):
            arrive(("c", s, by), factor.at[s, :, turn(x, -by, X), 1 - core], dcore=1)
        b_high, b_low = split(factor[s].reshape(W, DEPTH))
        product = dot3(a_high[...], a_low[...], b_high, b_low, ((1,), (1,)))
        partial[s] = product.reshape(ZL, Y, OUT, W)
        if s in Z_FIRST:
            for group in range(5):
                for by in GROUPS[group]:
                    for o in (1, 2):
                        source = partial.at[s, turn(zl, o, ZL), turn(y, by, Y)]
                        send(("z", s, by, o), source, whole_in.at[Z_FIRST.index(s), o - 1, turn(y, by, Y)], dzl=o)
        else:
            for part in range(ZL):
                start_y(s, part)

    def start_y(s, part):
        for at, way, rows in ((0, 1, slice(0, 8)), (1, -1, slice(8, 16))):
            source = partial.at[s, turn(zl, part + 1, ZL), turn(y, 4, Y), rows]
            send(("r", s, part, 0, way), source, half_in.at[s, part, at], dy=way)

    def reduce_z(s, group):
        for by in GROUPS[group]:
            d = turn(y, by, Y)
            for o in (1, 2):
                arrive(("z", s, by, o), whole_in.at[Z_FIRST.index(s), o - 1, d], dzl=o)
            partial[s, zl, d] += whole_in[Z_FIRST.index(s), 0, d] + whole_in[Z_FIRST.index(s), 1, d]
        if group == 0:
            start_y(s, ZL - 1)

    def reduce_y(s, part, step):
        to = turn(zl, part + 1, ZL)
        for at, way, rows in ((0, 1, slice(0, 8)), (1, -1, slice(8, 16))):
            if step == 0:
                arrive(("r", s, part, 0, way), half_in.at[s, part, at], dy=way)
                partial[s, to, turn(y, 3 * way, Y), rows] += half_in[s, part, at]
            else:
                arrive(("r", s, part, step, way), step_in.at[s, part, at, step - 1], dy=way)
                partial[s, to, turn(y, (3 - step) * way, Y)] += step_in[s, part, at, step - 1]
            if step < 3:
                source = partial.at[s, to, turn(y, (3 - step) * way, Y)]
                send(("r", s, part, step + 1, way), source, step_in.at[s, part, at, step], dy=way)
        if step == 3 and part < ZL - 1:
            send(("w", s, part + 1), partial.at[s, to, y], last_in.at[s, part], dzl=part + 1)

    def finish(s):
        total = partial[s, zl, y]
        if s not in Z_FIRST:
            for o in (1, 2):
                arrive(("w", s, o), last_in.at[s, o - 1], dzl=o)
            total = total + (last_in[s, 0] + last_in[s, 1])
        if s:
            total = total + o_ref[s]
        total = -total
        o_ref[s] = total
        if s + 1 < S:
            high, low = split(total)
            o_ref[s + 1] = dot3(high, low, k_high[s], k_low[s], ((1,), (0,)))

    def prepare():
        fill_a.wait()
        fill_k.wait()
        a_high[...], a_low[...] = split(a_ref[...])
        k_high[...], k_low[...] = split(k_ref[...])

    events = (
        prepare, gather_y, pick, own, from_zh, to_core, multiply, reduce_z, reduce_y, finish,
    )
    for what, *given in ORDER:
        events[what](*given)
    for made in unsent:
        made.wait_send()


def fused(table, inverse_tiles, factor_panels, couplings):
    vmem = pl.BlockSpec(memory_space=pltpu.VMEM)
    anywhere = pl.BlockSpec(memory_space=pl.ANY)
    return pl.pallas_call(
        kernel,
        out_shape=jax.ShapeDtypeStruct((S, OUT, W), F32),
        in_specs=[pl.BlockSpec(memory_space=pltpu.SMEM), anywhere, vmem, anywhere],
        out_specs=vmem,
        scratch_shapes=[
            pltpu.VMEM((ROWS, DEPTH), F32),
            pltpu.VMEM((S - 1, W, W), F32),
            pltpu.VMEM((S, 2, WP, 128), F32),
            pltpu.VMEM((Y, 2, WP, 128), F32),
            pltpu.VMEM((Y, 2, WP, 128), F32),
            pltpu.VMEM((Y, 2, WP, 128), F32),
            pltpu.VMEM((S, ZL, WP, DEPTH), F32),
            pltpu.VMEM((S, 2, WP, DEPTH), F32),
            pltpu.VMEM((S, ZH, X, CORE, WP, DEPTH), F32),
            pltpu.VMEM((S, ZL, Y, OUT, W), F32),
            pltpu.VMEM((S, ZL, 2, OUT // 2, W), F32),
            pltpu.VMEM((S, ZL, 2, 3, OUT, W), F32),
            pltpu.VMEM((max(1, len(Z_FIRST)), 2, Y, OUT, W), F32),
            pltpu.VMEM((S, 2, OUT, W), F32),
            pltpu.VMEM((ROWS, DEPTH), BF16),
            pltpu.VMEM((ROWS, DEPTH), BF16),
            pltpu.VMEM((S - 1, W, W), BF16),
            pltpu.VMEM((S - 1, W, W), BF16),
            pltpu.SemaphoreType.DMA((2,)),
            pltpu.SemaphoreType.DMA((COPIES,)),
            pltpu.SemaphoreType.DMA((COPIES,)),
        ],
        compiler_params=pltpu.CompilerParams(
            collective_id=0, has_side_effects=True, vmem_limit_bytes=60 * 1024 * 1024
        ),
    )(table, inverse_tiles, factor_panels, couplings)


def on_device(inverse_tiles, factor_panels, block_rows, couplings):
    col = lax.axis_index("col")
    zl, y = col // Y, lax.rem(col, Y)
    target = jnp.arange(TARGETS, dtype=jnp.int32)
    wanted = (target // NBC * Y + y) * NBC + target % NBC
    number = jnp.arange(1, NZB + 1, dtype=jnp.int32)
    found = jnp.sum(
        jnp.where(block_rows[:, :, None] == wanted, number[:, None], 0), axis=1
    )
    local = found - 1 - zl * (Y * LISTED)
    here = (found > 0) & (local >= 0) & (local < Y * LISTED)
    local = jnp.where(here, local, 0)
    shift = jnp.where(here, (target - local) % QUAD * RB, 0)
    place = jnp.where(here, target % QUAD, QUAD)
    table = jnp.stack([local // QUAD, shift, place], axis=-1).reshape(-1)
    return fused(table, inverse_tiles, factor_panels, couplings)


def solution(mesh):
    return jax.shard_map(
        on_device,
        mesh=mesh,
        in_specs=(P("row", "col"), P(None, "row", "col"), P(), P()),
        out_specs=P(None, ("row", "col"), None),
        check_vma=False,
    )
```

time: 674 us -> 85 us (0.13)
  the two profiles are of different devices: /device:TPU:192 before, /device:TPU:24 now
where the time goes in v1:
time: 85 us; the launch traced here: 84.8 us
  Pallas kernels  81.4 us (96%)
  local copies, waits for them, and re-layouts  2.43 us (3%)
  other arithmetic  0.94 us (1%)
    pallas_call x1, Pallas kernels, fused(): pl.pallas_call(kernel, out_shape=jax.ShapeDtypeStruct((S, OUT, W), F32),...  81.4 us

profile of v1, /device:TPU:24, one launch (start us, length us, event | category | flops | bytes accessed | tf_op | source)
XLA Modules:
  0.0 84.8 jit_solution(14590187079578086261)
XLA Ops:
  0.0 0.9 %select_reduce_fusion = s32[3,48]{1,0:T(4,128)S(1)} fusion(s32[192]{0:T(256)S(1)} %iota_add_fusion, s32[3,192]{1,0:T(4,128)} %param.6, s32[48]{0:T(128)S(1)} %fusion.7), kind=kLoop, calls=%fused_computation | loop fusion | flops 82800 | bytes 3840 | tf_op jit(solution)/shard_map/reduce_sum | solution.py:262
  1.0 0.1 copy.6
  1.1 0.8 reshape.182.table
  1.9 81.4 %shard_map.46 = f32[3,16,512]{2,1,0:T(8,128)} custom-call(s32[432]{0:T(512)} %reshape.182.table, f32[384,512]{1,0:T(8,128)} %a_hbm.1, f32[3,16,256]{2,1,0:T(8,128)} %f_ref.1, f32[2,512,512]{2,1,0:T(8,128)} %k_hbm.1), custom_call_target="tpu_custom_call" | custom-call | tf_op jit(solution)/shard_map/pallas_call | solution.py:222
  83.2 1.5 %copy.8 = f32[3,16,512]{2,1,0:T(8,128)} copy(f32[3,16,512]{2,1,0:T(8,128)} %shard_map.46) | data formatting | bytes 196608
  (5 shorter events, 0.0 us)

commit v2 on v1

v2 whole, which is shorter than its diff:
```python
import jax
import jax.numpy as jnp
from jax import lax
from jax.experimental import pallas as pl
from jax.experimental.pallas import tpu as pltpu
from jax.sharding import PartitionSpec as P

ZH, X, CORE, ZL, Y = 4, 4, 2, 3, 8
S, W, RB, NBC, NZB = 3, 512, 32, 16, 192
WP = W // (ZH * X * CORE)
LISTED = NZB // (ZL * Y)
ROWS, DEPTH = 384, 512
OUT = ROWS // (ZL * Y)
TARGETS = ZL * NBC
WZ = W // ZH
QUAD = 128 // RB
MESH = pl.DeviceIdType.MESH
F32, BF16 = jnp.float32, jnp.bfloat16
SENDS, ARRIVALS = 9, 78
PARTS = ((0,), (1, 3), (2,))
STEPS = tuple(o for part in PARTS for o in part)
HOP_ORDER = ((1, 3, 2), (1, 3, 2), (1, 3, 2))
ORDER = (
    (1, 0), (1, 1), (0,), (1, 2), (2, 0), (2, 1), (3, 0), (2, 2), (3, 1), (5, 0, 0), (6, 0, 0), (4, 0, 1),
    (4, 0, 3), (5, 1, 0), (6, 1, 0), (7, 0, 0, 0), (3, 2), (4, 0, 2), (4, 1, 1), (4, 1, 3), (5, 0, 1),
    (7, 1, 0, 0), (7, 0, 0, 1), (5, 2, 0), (6, 0, 1), (5, 0, 2), (6, 2, 0), (7, 1, 0, 1), (4, 1, 2),
    (4, 2, 1), (7, 0, 0, 2), (4, 2, 3), (6, 0, 2), (7, 0, 1, 0), (5, 1, 1), (7, 2, 0, 0), (7, 1, 0, 2),
    (7, 0, 0, 3), (4, 2, 2), (7, 0, 2, 0), (6, 1, 1), (5, 1, 2), (7, 0, 1, 1), (7, 2, 0, 1), (6, 1, 2),
    (8, 0, 0), (7, 0, 2, 1), (7, 1, 0, 3), (5, 2, 1), (7, 1, 1, 0), (5, 2, 2), (7, 0, 1, 2), (6, 2, 1),
    (6, 2, 2), (7, 1, 2, 0), (7, 0, 2, 2), (7, 2, 0, 2), (7, 1, 1, 1), (7, 0, 1, 3), (7, 2, 1, 0),
    (7, 2, 2, 0), (7, 1, 2, 1), (7, 0, 2, 3), (7, 2, 0, 3), (7, 1, 1, 2), (8, 0, 1), (7, 2, 1, 1),
    (7, 2, 2, 1), (8, 0, 2), (9, 0), (8, 1, 0), (7, 1, 2, 2), (7, 1, 1, 3), (7, 2, 1, 2), (7, 2, 2, 2),
    (7, 1, 2, 3), (8, 1, 1), (7, 2, 1, 3), (7, 2, 2, 3), (8, 1, 2), (9, 1), (8, 2, 0), (8, 2, 1), (8, 2, 2),
)


def split(value):
    high = value.astype(BF16)
    return high, (value - high.astype(F32)).astype(BF16)


def dot3(a_high, a_low, b_high, b_low, dims):
    def one(a, b):
        return lax.dot_general(a, b, (dims, ((), ())), preferred_element_type=F32)

    return one(a_high, b_high) + (one(a_high, b_low) + one(a_low, b_high))


def kernel(
    table, a_hbm, f_hbm, k_hbm, o_ref,
    a_ref, k_ref, f_own, listed_0, listed_1, listed_2, picked, from_zl, factor, partial,
    half_in, step_in, last_in, a_high, a_low, k_high, k_low, fill_sem, send_sem, recv_sem,
):
    row, col = lax.axis_index("row"), lax.axis_index("col")
    zh, x, core = row // (X * CORE), lax.rem(row // CORE, X), lax.rem(row, CORE)
    zl, y = col // Y, lax.rem(col, Y)
    listed = (listed_0, listed_1, listed_2)

    def turn(value, by, size):
        return lax.rem(value + (by + size), size)

    def device(dzh=0, dx=0, dcore=0, dzl=0, dy=0):
        at_row = (turn(zh, dzh, ZH) * X + turn(x, dx, X)) * CORE + (1 - core if dcore else core)
        return (at_row, turn(zl, dzl, ZL) * Y + turn(y, dy, Y))

    fill_f = [
        pltpu.make_async_copy(f_hbm.at[:, :, pl.ds(h * 128, 128)], f_own.at[:, h], fill_sem.at[h])
        for h in range(2)
    ]
    fill_a = pltpu.make_async_copy(a_hbm, a_ref, fill_sem.at[2])
    fill_k = pltpu.make_async_copy(k_hbm, k_ref, fill_sem.at[3])
    for fill in (*fill_f, fill_a, fill_k):
        fill.start()

    barrier = pltpu.get_barrier_semaphore()
    partners = (
        [dict(dy=o) for o in range(1, Y)]
        + [dict(dzl=o) for o in range(1, ZL)]
        + [dict(dzh=o) for o in range(1, ZH)]
        + [dict(dx=1), dict(dx=-1), dict(dx=2), dict(dcore=1)]
    )
    for partner in partners:
        pl.semaphore_signal(barrier, inc=1, device_id=device(**partner), device_id_type=MESH)
    for fill in fill_f:
        fill.wait()
    pl.semaphore_wait(barrier, len(partners))

    arrivals, sends = {}, {}

    def copy(sent, key, source, target, to):
        out, into = sends.setdefault(sent, len(sends)), arrivals.setdefault(key, len(arrivals))
        return pltpu.make_async_remote_copy(
            src_ref=source, dst_ref=target, send_sem=send_sem.at[out], recv_sem=recv_sem.at[into],
            device_id=to, device_id_type=MESH,
        )

    def send(sent, key, source, target, **to):
        copy(sent, key, source, target, device(**to)).start()

    def arrive(key, landed):
        copy(("y", 0), key, landed, landed, device(dcore=1)).wait_recv()

    def all_sent(sent, as_large):
        copy(sent, ("y", 0), as_large, as_large, device(dcore=1)).wait_send()

    lane_block = lax.broadcasted_iota(jnp.int32, (WP, 128), 1) // RB

    def gather_y(s):
        for o in (4, 3, 5, 2, 6, 1, 7):
            send(("y", s), ("y", s), f_own.at[s], listed[s].at[o - 1], dy=o)
        for h in range(2):
            listed[s][Y - 1, h] = f_own[s, h]

    def pick(s):
        arrive(("y", s), listed[s].at[0 : Y - 1])
        for part in range(ZL):
            for quad in range(NBC // QUAD):
                value = jnp.zeros((WP, 128), F32)
                for q in range(QUAD):
                    code = table[s, part * NBC + quad * QUAD + q]
                    tile = lax.min(code // QUAD, 2 * Y - 1)
                    shift = lax.rem(q + QUAD - lax.rem(code, QUAD), QUAD) * RB
                    place = jnp.where(code < Y * LISTED, q, QUAD)
                    block = pltpu.roll(listed[s][tile // 2, lax.rem(tile, 2)], shift, 1)
                    value = jnp.where(lane_block == place, block, value)
                picked[s, part, :, quad * 128 : (quad + 1) * 128] = value
        for o in (1, 2):
            send("l", ("l", s), picked.at[s, turn(zl, o, ZL)], from_zl.at[s, o - 1], dzl=o)

    def slots(part):
        first = STEPS.index(PARTS[part][0])
        return slice(first, first + len(PARTS[part]))

    def own(s):
        arrive(("l", s), from_zl.at[s])
        factor[s, 0, x, core] = picked[s, zl] + (from_zl[s, 0] + from_zl[s, 1])
        for o in HOP_ORDER[s]:
            send("h", ("h", s, o), factor.at[s, 0, x, core], factor.at[s, STEPS.index(o), x, core], dzh=o)
        along_x(s, 0)

    def along_x(s, o):
        piece = factor.at[s, STEPS.index(o), x, core]
        part = [o in steps for steps in PARTS].index(True)
        for by in (2, 1, -1):
            send("x", ("x", s, part), piece, piece, dx=by)

    def from_zh(s, o):
        arrive(("h", s, o), factor.at[s, STEPS.index(o), x, core])
        along_x(s, o)

    def to_core(s, part):
        arrive(("x", s, part), factor.at[s, slots(part), 0 : X - 1, core])
        pieces = factor.at[s, slots(part), :, core]
        send("c", ("c", s, part), pieces, pieces, dcore=1)

    def multiply(s, part):
        arrive(("c", s, part), factor.at[s, slots(part), :, 1 - core])
        count = len(PARTS[part])
        b_high, b_low = split(factor[s, slots(part)].reshape(count * WZ, DEPTH))
        product = dot3(a_high[...], a_low[...], b_high, b_low, ((1,), (1,)))
        for n in range(count):
            columns = product[:, n * WZ : (n + 1) * WZ]
            partial[s, slots(part).start + n] = columns.reshape(ZL, Y, OUT, WZ)
        for at, way, rows in ((0, 1, slice(0, 8)), (1, -1, slice(8, 16))):
            source = partial.at[s, slots(part), :, turn(y, 4, Y), rows]
            send("r", ("r", s, part, 0), source, half_in.at[s, at, slots(part)], dy=way)

    def reduce_y(s, part, step):
        at_part = slots(part)
        if step == 0:
            arrive(("r", s, part, 0), half_in.at[s, :, at_part])
        else:
            arrive(("r", s, part, step), step_in.at[s, step - 1, :, at_part])
        for at, way, rows in ((0, 1, slice(0, 8)), (1, -1, slice(8, 16))):
            if step == 0:
                partial[s, at_part, :, turn(y, 3 * way, Y), rows] += half_in[s, at, at_part]
            else:
                partial[s, at_part, :, turn(y, (3 - step) * way, Y)] += step_in[s, step - 1, at, at_part]
            if step < 3:
                source = partial.at[s, at_part, :, turn(y, (3 - step) * way, Y)]
                send("r", ("r", s, part, step + 1), source, step_in.at[s, step, at, at_part], dy=way)
        if step == 3:
            for o in (1, 2):
                source = partial.at[s, at_part, turn(zl, o, ZL), y]
                send("w", ("w", s, part), source, last_in.at[s, o - 1, at_part], dzl=o)

    def finish(s, part):
        arrive(("w", s, part), last_in.at[s, :, slots(part)])
        for o in PARTS[part]:
            at = STEPS.index(o)
            columns = pl.ds(pl.multiple_of(turn(zh, -o, ZH) * WZ, WZ), WZ)
            total = partial[s, at, zl, y] + (last_in[s, 0, at] + last_in[s, 1, at])
            if s:
                total = total + o_ref[s, :, columns]
            o_ref[s, :, columns] = -total

    def couple(s):
        high, low = split(o_ref[s])
        o_ref[s + 1] = dot3(high, low, k_high[s], k_low[s], ((1,), (0,)))

    def prepare():
        fill_a.wait()
        fill_k.wait()
        a_high[...], a_low[...] = split(a_ref[...])
        k_high[...], k_low[...] = split(k_ref[...])

    events = (
        prepare, gather_y, pick, own, from_zh, to_core, multiply, reduce_y, finish, couple,
    )
    for what, *given in ORDER:
        events[what](*given)
    all_sent("l", from_zl)
    all_sent("h", picked)
    all_sent("x", factor.at[:, :, 0:3, 0])
    all_sent("c", factor.at[:, :, :, 0])
    for s in range(S):
        all_sent(("y", s), listed[s].at[0 : Y - 1])
    all_sent("r", partial.at[:, :, :, 0 : Y - 1])
    all_sent("w", last_in)
    assert (len(sends), len(arrivals)) == (SENDS, ARRIVALS)


def fused(table, inverse_tiles, factor_panels, couplings):
    hbm = pl.BlockSpec(memory_space=pltpu.HBM)
    return pl.pallas_call(
        kernel,
        out_shape=jax.ShapeDtypeStruct((S, OUT, W), F32),
        in_specs=[pl.BlockSpec(memory_space=pltpu.SMEM), hbm, hbm, hbm],
        out_specs=pl.BlockSpec(memory_space=pltpu.VMEM),
        scratch_shapes=[
            pltpu.VMEM((ROWS, DEPTH), F32),
            pltpu.VMEM((S - 1, W, W), F32),
            pltpu.VMEM((S, 2, WP, 128), F32),
            pltpu.VMEM((Y, 2, WP, 128), F32),
            pltpu.VMEM((Y, 2, WP, 128), F32),
            pltpu.VMEM((Y, 2, WP, 128), F32),
            pltpu.VMEM((S, ZL, WP, DEPTH), F32),
            pltpu.VMEM((S, 2, WP, DEPTH), F32),
            pltpu.VMEM((S, ZH, X, CORE, WP, DEPTH), F32),
            pltpu.VMEM((S, ZH, ZL, Y, OUT, WZ), F32),
            pltpu.VMEM((S, 2, ZH, ZL, OUT // 2, WZ), F32),
            pltpu.VMEM((S, 3, 2, ZH, ZL, OUT, WZ), F32),
            pltpu.VMEM((S, 2, ZH, OUT, WZ), F32),
            pltpu.VMEM((ROWS, DEPTH), BF16),
            pltpu.VMEM((ROWS, DEPTH), BF16),
            pltpu.VMEM((S - 1, W, W), BF16),
            pltpu.VMEM((S - 1, W, W), BF16),
            pltpu.SemaphoreType.DMA((4,)),
            pltpu.SemaphoreType.DMA((SENDS,)),
            pltpu.SemaphoreType.DMA((ARRIVALS,)),
        ],
        compiler_params=pltpu.CompilerParams(
            collective_id=0, has_side_effects=True, vmem_limit_bytes=60 * 1024 * 1024
        ),
    )(table, inverse_tiles, factor_panels, couplings)


def on_device(inverse_tiles, factor_panels, block_rows, couplings):
    col = lax.axis_index("col")
    zl, y = col // Y, lax.rem(col, Y)
    target = jnp.arange(TARGETS, dtype=jnp.int32)
    wanted = (target // NBC * Y + y) * NBC + target % NBC
    number = jnp.arange(1, NZB + 1, dtype=jnp.int32)
    found = jnp.sum(
        jnp.where(block_rows[:, :, None] == wanted, number[:, None], 0), axis=1
    )
    local = found - 1 - zl * (Y * LISTED)
    here = (found > 0) & (local >= 0) & (local < Y * LISTED)
    slot = (y + (Y - 1) - local // LISTED) % Y
    code = jnp.where(here, slot * LISTED + local % LISTED, Y * LISTED)
    return fused(code, inverse_tiles, factor_panels, couplings)


def solution(mesh):
    return jax.shard_map(
        on_device,
        mesh=mesh,
        in_specs=(P("row", "col"), P(None, "row", "col"), P(), P()),
        out_specs=P(None, ("row", "col"), None),
        check_vma=False,
    )
```

time: 85 us -> 79.7 us (0.938)
  the two profiles are of different devices: /device:TPU:24 before, /device:TPU:8 now
where the time goes in v2:
time: 79.7 us; the launch traced here: 79.4 us
  Pallas kernels  76.4 us (96%)
  local copies, waits for them, and re-layouts  1.54 us (2%)
  other arithmetic  1.52 us (2%)
    pallas_call x1, Pallas kernels, fused(): pl.pallas_call(kernel, out_shape=jax.ShapeDtypeStruct((S, OUT, W), F32),...  76.4 us

profile of v2, /device:TPU:8, one launch (start us, length us, event | category | flops | bytes accessed | tf_op | source)
XLA Modules:
  0.0 79.4 jit_solution(36371614514518443)
XLA Ops:
  0.0 0.9 %select_reduce_fusion = s32[3,48]{1,0:T(4,128)S(1)} fusion(s32[192]{0:T(256)S(1)} %iota_add_fusion, s32[3,192]{1,0:T(4,128)} %param.6, s32[48]{0:T(128)S(1)} %fusion.6), kind=kLoop, calls=%fused_computation | loop fusion | flops 82800 | bytes 3840 | tf_op jit(solution)/shard_map/reduce_sum | solution.py:264
  0.9 0.6 fusion.4.table
  1.5 76.4 %shard_map.46 = f32[3,16,512]{2,1,0:T(8,128)} custom-call(s32[3,48]{1,0:T(4,128)} %fusion.4.table, f32[384,512]{1,0:T(8,128)} %a_hbm.1, f32[3,16,256]{2,1,0:T(8,128)} %f_hbm.1, f32[2,512,512]{2,1,0:T(8,128)} %k_hbm.1), custom_call_target="tpu_custom_call" | custom-call | tf_op jit(solution)/shard_map/pallas_call | solution.py:225
  77.9 1.5 %copy.6 = f32[3,16,512]{2,1,0:T(8,128)} copy(f32[3,16,512]{2,1,0:T(8,128)} %shard_map.46) | data formatting | bytes 196608
  (2 shorter events, 0.0 us)

commit v3 on v2

--- a/solution.py
+++ b/solution.py
@@ -19,18 +19,18 @@
 SENDS, ARRIVALS = 9, 78
 PARTS = ((0,), (1, 3), (2,))
 STEPS = tuple(o for part in PARTS for o in part)
-HOP_ORDER = ((1, 3, 2), (1, 3, 2), (1, 3, 2))
+RELAYED = (0, 1, 2)
 ORDER = (
-    (1, 0), (1, 1), (0,), (1, 2), (2, 0), (2, 1), (3, 0), (2, 2), (3, 1), (5, 0, 0), (6, 0, 0), (4, 0, 1),
-    (4, 0, 3), (5, 1, 0), (6, 1, 0), (7, 0, 0, 0), (3, 2), (4, 0, 2), (4, 1, 1), (4, 1, 3), (5, 0, 1),
-    (7, 1, 0, 0), (7, 0, 0, 1), (5, 2, 0), (6, 0, 1), (5, 0, 2), (6, 2, 0), (7, 1, 0, 1), (4, 1, 2),
-    (4, 2, 1), (7, 0, 0, 2), (4, 2, 3), (6, 0, 2), (7, 0, 1, 0), (5, 1, 1), (7, 2, 0, 0), (7, 1, 0, 2),
-    (7, 0, 0, 3), (4, 2, 2), (7, 0, 2, 0), (6, 1, 1), (5, 1, 2), (7, 0, 1, 1), (7, 2, 0, 1), (6, 1, 2),
-    (8, 0, 0), (7, 0, 2, 1), (7, 1, 0, 3), (5, 2, 1), (7, 1, 1, 0), (5, 2, 2), (7, 0, 1, 2), (6, 2, 1),
-    (6, 2, 2), (7, 1, 2, 0), (7, 0, 2, 2), (7, 2, 0, 2), (7, 1, 1, 1), (7, 0, 1, 3), (7, 2, 1, 0),
-    (7, 2, 2, 0), (7, 1, 2, 1), (7, 0, 2, 3), (7, 2, 0, 3), (7, 1, 1, 2), (8, 0, 1), (7, 2, 1, 1),
-    (7, 2, 2, 1), (8, 0, 2), (9, 0), (8, 1, 0), (7, 1, 2, 2), (7, 1, 1, 3), (7, 2, 1, 2), (7, 2, 2, 2),
-    (7, 1, 2, 3), (8, 1, 1), (7, 2, 1, 3), (7, 2, 2, 3), (8, 1, 2), (9, 1), (8, 2, 0), (8, 2, 1), (8, 2, 2),
+    (1, 0), (1, 2), (0,), (1, 1), (2, 0), (2, 2), (3, 0), (2, 1), (3, 2), (5, 0, 0), (6, 0, 0), (4, 0, 3),
+    (4, 0, 1), (5, 2, 0), (3, 1), (6, 2, 0), (7, 0, 0, 0), (4, 2, 1), (4, 2, 3), (4, 0, 2), (5, 0, 1),
+    (7, 2, 0, 0), (7, 0, 0, 1), (5, 1, 0), (4, 1, 3), (4, 1, 1), (6, 0, 1), (4, 2, 2), (6, 1, 0),
+    (7, 0, 0, 2), (5, 2, 1), (7, 2, 0, 1), (5, 0, 2), (7, 0, 1, 0), (4, 1, 2), (6, 2, 1), (6, 0, 2),
+    (7, 2, 0, 2), (7, 0, 0, 3), (7, 1, 0, 0), (5, 1, 1), (7, 0, 1, 1), (5, 2, 2), (5, 1, 2), (7, 2, 1, 0),
+    (7, 0, 2, 0), (6, 1, 1), (6, 1, 2), (7, 1, 0, 1), (7, 0, 1, 2), (8, 0, 0), (6, 2, 2), (7, 0, 2, 1),
+    (7, 1, 1, 0), (7, 2, 1, 1), (7, 1, 2, 0), (7, 2, 0, 3), (7, 1, 0, 2), (7, 0, 1, 3), (7, 2, 2, 0),
+    (7, 0, 2, 2), (7, 1, 1, 1), (7, 2, 1, 2), (7, 1, 2, 1), (8, 0, 1), (7, 1, 0, 3), (7, 2, 2, 1),
+    (7, 0, 2, 3), (7, 1, 1, 2), (7, 2, 1, 3), (7, 1, 2, 2), (7, 2, 2, 2), (8, 0, 2), (9, 0), (8, 1, 0),
+    (7, 1, 1, 3), (7, 1, 2, 3), (7, 2, 2, 3), (8, 1, 1), (8, 1, 2), (9, 1), (8, 2, 1), (8, 2, 2), (8, 2, 0),
 )
 
 
@@ -134,7 +134,7 @@
     def own(s):
         arrive(("l", s), from_zl.at[s])
         factor[s, 0, x, core] = picked[s, zl] + (from_zl[s, 0] + from_zl[s, 1])
-        for o in HOP_ORDER[s]:
+        for o in (1, 3) if s in RELAYED else (1, 3, 2):
             send("h", ("h", s, o), factor.at[s, 0, x, core], factor.at[s, STEPS.index(o), x, core], dzh=o)
         along_x(s, 0)
 
@@ -146,6 +146,10 @@
 
     def from_zh(s, o):
         arrive(("h", s, o), factor.at[s, STEPS.index(o), x, core])
+        if s in RELAYED and o != 2:
+            half = slice(0, WP // 2) if o == 1 else slice(WP // 2, WP)
+            source = factor.at[s, STEPS.index(o), x, core, half]
+            send("h", ("h", s, 2), source, factor.at[s, STEPS.index(2), x, core, half], dzh=o)
         along_x(s, o)
 
     def to_core(s, part):

time: 79.7 us -> 78.1 us (0.980)
  Pallas kernels: 76.4 us -> 74.8 us
    pallas_call x1, Pallas kernels: 76.4 us -> 74.8 us  [fused(): pl.pallas_call(kernel, out_shape=jax.ShapeDtypeStruct((S, OUT, W), F32),...]
where the time goes in v3:
time: 78.1 us; the launch traced here: 77.8 us
  Pallas kernels  74.8 us (96%)
  local copies, waits for them, and re-layouts  1.54 us (2%)
  other arithmetic  1.52 us (2%)
    pallas_call x1, Pallas kernels, fused(): pl.pallas_call(kernel, out_shape=jax.ShapeDtypeStruct((S, OUT, W), F32),...  74.8 us

profile of v3, /device:TPU:8, one launch (start us, length us, event | category | flops | bytes accessed | tf_op | source)
XLA Modules:
  0.0 77.8 jit_solution(5102778419883113289)
XLA Ops:
  0.0 0.9 %select_reduce_fusion = s32[3,48]{1,0:T(4,128)S(1)} fusion(s32[192]{0:T(256)S(1)} %iota_add_fusion, s32[3,192]{1,0:T(4,128)} %param.6, s32[48]{0:T(128)S(1)} %fusion.6), kind=kLoop, calls=%fused_computation | loop fusion | flops 82800 | bytes 3840 | tf_op jit(solution)/shard_map/reduce_sum | solution.py:268
  0.9 0.6 fusion.4.table
  1.5 74.8 %shard_map.46 = f32[3,16,512]{2,1,0:T(8,128)} custom-call(s32[3,48]{1,0:T(4,128)} %fusion.4.table, f32[384,512]{1,0:T(8,128)} %a_hbm.1, f32[3,16,256]{2,1,0:T(8,128)} %f_hbm.1, f32[2,512,512]{2,1,0:T(8,128)} %k_hbm.1), custom_call_target="tpu_custom_call" | custom-call | tf_op jit(solution)/shard_map/pallas_call | solution.py:229
  76.3 1.5 %copy.6 = f32[3,16,512]{2,1,0:T(8,128)} copy(f32[3,16,512]{2,1,0:T(8,128)} %shard_map.46) | data formatting | bytes 196608
  (2 shorter events, 0.0 us)

commit v4 on v3

--- a/solution.py
+++ b/solution.py
@@ -266,7 +266,7 @@
     wanted = (target // NBC * Y + y) * NBC + target % NBC
     number = jnp.arange(1, NZB + 1, dtype=jnp.int32)
     found = jnp.sum(
-        jnp.where(block_rows[:, :, None] == wanted, number[:, None], 0), axis=1
+        jnp.where(block_rows[:, None, :] == wanted[:, None], number, 0), axis=2
     )
     local = found - 1 - zl * (Y * LISTED)
     here = (found > 0) & (local >= 0) & (local < Y * LISTED)

time: 78.1 us -> 78.1 us (level)
  no operation moved by 1% of the time
where the time goes in v4:
time: 78.1 us; the launch traced here: 77.8 us
  Pallas kernels  74.8 us (96%)
  local copies, waits for them, and re-layouts  1.54 us (2%)
  other arithmetic  1.52 us (2%)
    pallas_call x1, Pallas kernels, fused(): pl.pallas_call(kernel, out_shape=jax.ShapeDtypeStruct((S, OUT, W), F32),...  74.8 us

profile of v4, /device:TPU:8, one launch (start us, length us, event | category | flops | bytes accessed | tf_op | source)
XLA Modules:
  0.0 77.8 jit_solution(5102778419883113289)
XLA Ops:
  0.0 0.9 %select_reduce_fusion = s32[3,48]{1,0:T(4,128)S(1)} fusion(s32[192]{0:T(256)S(1)} %iota_add_fusion, s32[3,192]{1,0:T(4,128)} %param.6, s32[48]{0:T(128)S(1)} %fusion.6), kind=kLoop, calls=%fused_computation | loop fusion | flops 82800 | bytes 3840 | tf_op jit(solution)/shard_map/reduce_sum | solution.py:268
  0.9 0.6 fusion.4.table
  1.5 74.8 %shard_map.46 = f32[3,16,512]{2,1,0:T(8,128)} custom-call(s32[3,48]{1,0:T(4,128)} %fusion.4.table, f32[384,512]{1,0:T(8,128)} %a_hbm.1, f32[3,16,256]{2,1,0:T(8,128)} %f_hbm.1, f32[2,512,512]{2,1,0:T(8,128)} %k_hbm.1), custom_call_target="tpu_custom_call" | custom-call | tf_op jit(solution)/shard_map/pallas_call | solution.py:229
  76.3 1.5 %copy.6 = f32[3,16,512]{2,1,0:T(8,128)} copy(f32[3,16,512]{2,1,0:T(8,128)} %shard_map.46) | data formatting | bytes 196608
  (2 shorter events, 0.0 us)
